TPU v7x, 32 devices: a whole 2x2x4 slice. The times are simulated.
32 devices in a mesh: dp: 4 (over x, core), mp: 8 (over z, y).
Axes of the slice: x: 2, y: 2, z: 4, core: 2. Of those that a mesh axis runs over, the one named last changes fastest.
Arguments:
- tokens: bfloat16 [4704, 768], P(('dp', 'mp')), may hold values from -6 to 6
- crop_kind: int32 [96], P('dp'), may hold values from 0 to 1, as said below
- norm1_gain: float32 [768], replicated, may hold values from 0.1 to 1.9
- norm1_bias: float32 [768], replicated, may hold values from -1.75 to 1.75
- qkv_weight: bfloat16 [3, 768, 768], P(None, None, 'mp'), may hold values from -0.21875 to 0.21875
- qv_bias: float32 [2, 768], P(None, 'mp'), may hold values from -3 to 3
- rel_table: float32 [169, 24], P(None, 'mp'), may hold values from -6 to 6
- proj_weight: bfloat16 [768, 768], P('mp'), may hold values from -0.875 to 0.875
- proj_bias: float32 [768], replicated, may hold values from -1.75 to 1.75
- norm2_gain: float32 [768], replicated, may hold values from 0.1 to 1.9
- norm2_bias: float32 [768], replicated, may hold values from -1.75 to 1.75
- fc1_weight: bfloat16 [768, 3072], P(None, 'mp'), may hold values from -0.21875 to 0.21875
- fc1_bias: float32 [3072], P('mp'), may hold values from -3 to 3
- fc2_weight: bfloat16 [3072, 768], P('mp'), may hold values from -0.109375 to 0.109375
- fc2_bias: float32 [768], replicated, may hold values from -1.75 to 1.75
- out_grad: bfloat16 [4704, 768], P(('dp', 'mp')), may hold values from -6 to 6
Outputs:
- block_out: bfloat16 [4704, 768], P(('dp', 'mp'))
- tokens_grad: bfloat16 [4704, 768], P(('dp', 'mp'))
- norm1_gain_grad: float32 [768], replicated
- norm1_bias_grad: float32 [768], replicated
- qkv_weight_grad: float32 [3, 768, 768], P(None, None, 'mp')
- qv_bias_grad: float32 [2, 768], P(None, 'mp')
- rel_table_grad: float32 [169, 24], P(None, 'mp')
- proj_weight_grad: float32 [768, 768], P('mp')
- proj_bias_grad: float32 [768], replicated
- norm2_gain_grad: float32 [768], replicated
- norm2_bias_grad: float32 [768], replicated
- fc1_weight_grad: float32 [768, 3072], P(None, 'mp')
- fc1_bias_grad: float32 [3072], P('mp')
- fc2_weight_grad: float32 [3072, 768], P('mp')
- fc2_bias_grad: float32 [768], replicated
Inputs may be any that keep to these rules, and one draw needn't show every extreme that they name: `crop_kind`: 0 marks a global crop, whose 49 slots all hold patches; 1 marks a local crop, whose first 9 slots hold patches. Both kinds occur.
All inputs are finite; a program needn't handle non-finite values.
Results may differ from a plain program's by a relative error of at most 0.024.
Values may be sent and summed in bfloat16 or wider, within the bound.
A program may use at most 64 MiB of HBM per device.

v0:
```python
import jax
import jax.numpy as jnp
from jax import lax
from jax.sharding import PartitionSpec as P

HEAD = 32
SIDE = 7
LOCAL_SIDE = 3
WIN = 49
EPSILON = 1e-05
NEG_FILL = -1000000000.0
HIGHEST = lax.Precision.HIGHEST


def normalize(values, gain_vec, shift_vec):
    centre = values - jnp.mean(values, axis=-1, keepdims=True)
    spread = jnp.mean(centre * centre, axis=-1, keepdims=True)
    return centre * lax.rsqrt(spread + EPSILON) * gain_vec + shift_vec


def gelu_tanh(values):
    return jax.nn.gelu(values, approximate=True)


def relative_index(side_len):
    slot_ids = jnp.minimum(jnp.arange(WIN), side_len * side_len - 1)
    slot_row = slot_ids // side_len
    slot_col = slot_ids % side_len
    offset_row = slot_row[:, None] - slot_row[None, :] + SIDE - 1
    offset_col = slot_col[:, None] - slot_col[None, :] + SIDE - 1
    return offset_row * (2 * SIDE - 1) + offset_col


def window_live(kinds):
    return jnp.where(kinds == 0, WIN, LOCAL_SIDE * LOCAL_SIDE)


def table_onehot():
    index_both = jnp.stack([relative_index(SIDE), relative_index(LOCAL_SIDE)]).reshape(2, WIN * WIN)
    entries = jnp.arange((2 * SIDE - 1) ** 2, dtype=jnp.int32)
    return (index_both[:, :, None] == entries[None, None, :]).astype(jnp.float32)


def dot_rows(left, right):
    return lax.dot_general(
        left, right, (((0,), (0,)), ((), ())), preferred_element_type=jnp.float32
    )


def dot_back(left, right):
    return lax.dot_general(
        left, right, (((1,), (1,)), ((), ())), preferred_element_type=jnp.float32
    )


def attention_scores(query_four, key_four, bias_win, key_usable):
    score_raw = jnp.einsum(
        "wqhd,wkhd->whqk", query_four, key_four, preferred_element_type=jnp.float32
    )
    return jnp.where(key_usable[:, None, None, :], score_raw + bias_win, NEG_FILL)


def forward_pass(inputs, kinds, row_live, params, onehot):
    (
        gain_one,
        shift_one,
        qkv_weight,
        qv_bias,
        rel_table,
        proj_weight,
        proj_bias,
        gain_two,
        shift_two,
        fc1_weight,
        fc1_bias,
        fc2_weight,
        fc2_bias,
    ) = params
    head_cols = qkv_weight.shape[2]
    heads_here = head_cols // HEAD
    windows = kinds.shape[0]
    normed_one = normalize(inputs, gain_one, shift_one).astype(jnp.bfloat16)
    rows_one = lax.all_gather(normed_one, "mp", axis=0, tiled=True)
    query_rows = (
        (jnp.dot(rows_one, qkv_weight[0], preferred_element_type=jnp.float32) + qv_bias[0])
        * HEAD ** (-0.5)
    ).astype(jnp.bfloat16)
    key_rows = jnp.dot(rows_one, qkv_weight[1], preferred_element_type=jnp.float32).astype(
        jnp.bfloat16
    )
    value_rows = (
        jnp.dot(rows_one, qkv_weight[2], preferred_element_type=jnp.float32) + qv_bias[1]
    ).astype(jnp.bfloat16)
    bias_both = jnp.einsum("kpt,th->khp", onehot, rel_table, precision=HIGHEST).reshape(
        2, heads_here, WIN, WIN
    )
    is_global = (kinds == 0)[:, None, None, None]
    bias_win = jnp.where(is_global, bias_both[0][None], bias_both[1][None])
    key_usable = jnp.arange(WIN)[None, :] < window_live(kinds)[:, None]
    win_shape = (windows, WIN, heads_here, HEAD)
    scores = attention_scores(
        query_rows.reshape(win_shape), key_rows.reshape(win_shape), bias_win, key_usable
    )
    row_max = jnp.max(scores, axis=-1, keepdims=True)
    log_total = row_max + jnp.log(jnp.sum(jnp.exp(scores - row_max), axis=-1, keepdims=True))
    prob_bf = jnp.exp(scores - log_total).astype(jnp.bfloat16)
    head_out = (
        jnp.einsum(
            "whqk,wkhd->wqhd",
            prob_bf,
            value_rows.reshape(win_shape),
            preferred_element_type=jnp.float32,
        )
        .reshape(windows * WIN, head_cols)
        .astype(jnp.bfloat16)
    )
    attn_branch = lax.psum_scatter(
        jnp.dot(head_out, proj_weight, preferred_element_type=jnp.float32).astype(jnp.bfloat16),
        "mp",
        scatter_dimension=0,
        tiled=True,
    ).astype(jnp.float32)
    middle = inputs + (attn_branch + proj_bias) * row_live
    normed_two = normalize(middle, gain_two, shift_two).astype(jnp.bfloat16)
    rows_two = lax.all_gather(normed_two, "mp", axis=0, tiled=True)
    hidden_pre = jnp.dot(rows_two, fc1_weight, preferred_element_type=jnp.float32) + fc1_bias
    hidden_act = gelu_tanh(hidden_pre).astype(jnp.bfloat16)
    mlp_branch = lax.psum_scatter(
        jnp.dot(hidden_act, fc2_weight, preferred_element_type=jnp.float32).astype(jnp.bfloat16),
        "mp",
        scatter_dimension=0,
        tiled=True,
    ).astype(jnp.float32)
    result = middle + (mlp_branch + fc2_bias) * row_live
    return (
        result,
        middle,
        rows_one,
        query_rows,
        key_rows,
        value_rows,
        bias_win,
        key_usable,
        log_total,
        head_out,
        rows_two,
        hidden_pre,
        hidden_act,
    )


def shards(
    tokens,
    crop_kind,
    norm1_gain,
    norm1_bias,
    qkv_weight,
    qv_bias,
    rel_table,
    proj_weight,
    proj_bias,
    norm2_gain,
    norm2_bias,
    fc1_weight,
    fc1_bias,
    fc2_weight,
    fc2_bias,
    out_grad,
):
    params = (
        norm1_gain,
        norm1_bias,
        qkv_weight,
        qv_bias,
        rel_table,
        proj_weight,
        proj_bias,
        norm2_gain,
        norm2_bias,
        fc1_weight,
        fc1_bias,
        fc2_weight,
        fc2_bias,
    )
    onehot = table_onehot()
    own_rows = tokens.shape[0]
    own_windows = own_rows // WIN
    own_kind = lax.dynamic_slice_in_dim(crop_kind, lax.axis_index("mp") * own_windows, own_windows)
    row_live = (
        (jnp.arange(WIN)[None, :] < window_live(own_kind)[:, None])
        .astype(jnp.float32)
        .reshape(own_rows, 1)
    )
    inputs = tokens.astype(jnp.float32)
    first_pass = forward_pass(inputs, crop_kind, row_live, params, onehot)
    block_out = first_pass[0].astype(jnp.bfloat16)
    saved = forward_pass(inputs, crop_kind, row_live, params, onehot)
    (
        unused_out,
        middle,
        rows_one,
        query_rows,
        key_rows,
        value_rows,
        bias_win,
        key_usable,
        log_total,
        head_out,
        rows_two,
        hidden_pre,
        hidden_act,
    ) = saved
    head_cols = qkv_weight.shape[2]
    heads_here = head_cols // HEAD
    windows = crop_kind.shape[0]
    win_shape = (windows, WIN, heads_here, HEAD)
    upstream = out_grad.astype(jnp.float32)
    mlp_grad = upstream * row_live
    fc2_bias_grad = jnp.sum(mlp_grad, axis=0)
    mlp_grad_rows = lax.all_gather(mlp_grad.astype(jnp.bfloat16), "mp", axis=0, tiled=True)
    fc2_weight_grad = dot_rows(hidden_act, mlp_grad_rows)
    act_grad = dot_back(mlp_grad_rows, fc2_weight)
    unused_act, gelu_pull = jax.vjp(gelu_tanh, hidden_pre)
    pre_grad = gelu_pull(act_grad)[0].astype(jnp.bfloat16)
    fc1_bias_grad = jnp.sum(pre_grad.astype(jnp.float32), axis=0)
    fc1_weight_grad = dot_rows(rows_two, pre_grad)
    normed_two_grad = lax.psum_scatter(
        dot_back(pre_grad, fc1_weight).astype(jnp.bfloat16), "mp", scatter_dimension=0, tiled=True
    ).astype(jnp.float32)
    unused_two, norm_two_pull = jax.vjp(normalize, middle, norm2_gain, norm2_bias)
    middle_grad, norm2_gain_grad, norm2_bias_grad = norm_two_pull(normed_two_grad)
    middle_grad = middle_grad + upstream
    attn_grad = middle_grad * row_live
    proj_bias_grad = jnp.sum(attn_grad, axis=0)
    attn_grad_rows = lax.all_gather(attn_grad.astype(jnp.bfloat16), "mp", axis=0, tiled=True)
    proj_weight_grad = dot_rows(head_out, attn_grad_rows)
    head_grad = dot_back(attn_grad_rows, proj_weight).astype(jnp.bfloat16).reshape(win_shape)
    query_four = query_rows.reshape(win_shape)
    key_four = key_rows.reshape(win_shape)
    scores = attention_scores(query_four, key_four, bias_win, key_usable)
    prob_full = jnp.exp(scores - log_total)
    prob_bf = prob_full.astype(jnp.bfloat16)
    prob_grad = jnp.einsum(
        "wqhd,wkhd->whqk",
        head_grad,
        value_rows.reshape(win_shape),
        preferred_element_type=jnp.float32,
    )
    value_grad = (
        jnp.einsum("whqk,wqhd->wkhd", prob_bf, head_grad, preferred_element_type=jnp.float32)
        .reshape(-1, head_cols)
        .astype(jnp.bfloat16)
    )
    score_grad = prob_full * (prob_grad - jnp.sum(prob_full * prob_grad, axis=-1, keepdims=True))
    is_global = (crop_kind == 0)[:, None, None, None]
    bias_grad = jnp.stack(
        [
            jnp.sum(jnp.where(is_global, score_grad, 0.0), axis=0),
            jnp.sum(jnp.where(is_global, 0.0, score_grad), axis=0),
        ]
    ).reshape(2, heads_here, WIN * WIN)
    rel_table_grad = jnp.einsum("kpt,khp->th", onehot, bias_grad, precision=HIGHEST)
    score_bf = score_grad.astype(jnp.bfloat16)
    query_grad = (
        jnp.einsum(
            "whqk,wkhd->wqhd", score_bf, key_four, preferred_element_type=jnp.float32
        ).reshape(-1, head_cols)
        * HEAD ** (-0.5)
    ).astype(jnp.bfloat16)
    key_grad = (
        jnp.einsum("whqk,wqhd->wkhd", score_bf, query_four, preferred_element_type=jnp.float32)
        .reshape(-1, head_cols)
        .astype(jnp.bfloat16)
    )
    qkv_weight_grad = jnp.stack(
        [
            dot_rows(rows_one, query_grad),
            dot_rows(rows_one, key_grad),
            dot_rows(rows_one, value_grad),
        ]
    )
    qv_bias_grad = jnp.stack(
        [
            jnp.sum(query_grad.astype(jnp.float32), axis=0),
            jnp.sum(value_grad.astype(jnp.float32), axis=0),
        ]
    )
    total = dot_back(query_grad, qkv_weight[0])
    total = total + dot_back(key_grad, qkv_weight[1])
    normed_one_grad = lax.psum_scatter(
        (total + dot_back(value_grad, qkv_weight[2])).astype(jnp.bfloat16),
        "mp",
        scatter_dimension=0,
        tiled=True,
    ).astype(jnp.float32)
    unused_one, norm_one_pull = jax.vjp(normalize, inputs, norm1_gain, norm1_bias)
    input_grad, norm1_gain_grad, norm1_bias_grad = norm_one_pull(normed_one_grad)
    tokens_grad = (input_grad + middle_grad).astype(jnp.bfloat16)
    small_grads = jnp.stack(
        [
            norm1_gain_grad,
            norm1_bias_grad,
            proj_bias_grad,
            norm2_gain_grad,
            norm2_bias_grad,
            fc2_bias_grad,
        ]
    )
    small_grads = lax.psum(small_grads, "mp")
    (
        qkv_weight_grad,
        qv_bias_grad,
        rel_table_grad,
        proj_weight_grad,
        fc1_weight_grad,
        fc1_bias_grad,
        fc2_weight_grad,
        small_grads,
    ) = (
        lax.psum(qkv_weight_grad.astype(jnp.bfloat16), "dp").astype(jnp.float32),
        lax.psum(qv_bias_grad.astype(jnp.bfloat16), "dp").astype(jnp.float32),
        lax.psum(rel_table_grad.astype(jnp.bfloat16), "dp").astype(jnp.float32),
        lax.psum(proj_weight_grad.astype(jnp.bfloat16), "dp").astype(jnp.float32),
        lax.psum(fc1_weight_grad.astype(jnp.bfloat16), "dp").astype(jnp.float32),
        lax.psum(fc1_bias_grad.astype(jnp.bfloat16), "dp").astype(jnp.float32),
        lax.psum(fc2_weight_grad.astype(jnp.bfloat16), "dp").astype(jnp.float32),
        lax.psum(small_grads.astype(jnp.bfloat16), "dp").astype(jnp.float32),
    )
    return (
        block_out,
        tokens_grad,
        small_grads[0],
        small_grads[1],
        qkv_weight_grad,
        qv_bias_grad,
        rel_table_grad,
        proj_weight_grad,
        small_grads[2],
        small_grads[3],
        small_grads[4],
        fc1_weight_grad,
        fc1_bias_grad,
        fc2_weight_grad,
        small_grads[5],
    )


def solution(mesh):
    in_specs = (
        P(("dp", "mp"), None),
        P("dp"),
        P(),
        P(),
        P(None, None, "mp"),
        P(None, "mp"),
        P(None, "mp"),
        P("mp", None),
        P(),
        P(),
        P(),
        P(None, "mp"),
        P("mp"),
        P("mp", None),
        P(),
        P(("dp", "mp"), None),
    )
    out_specs = (
        P(("dp", "mp"), None),
        P(("dp", "mp"), None),
        P(),
        P(),
        P(None, None, "mp"),
        P(None, "mp"),
        P(None, "mp"),
        P("mp", None),
        P(),
        P(),
        P(),
        P(None, "mp"),
        P("mp"),
        P("mp", None),
        P(),
    )
    return jax.shard_map(shards, mesh=mesh, in_specs=in_specs, out_specs=out_specs, check_vma=False)
```

profile of v0, /device:TPU:0, one launch (start us, length us, event | category | flops | bytes accessed | tf_op | source)
XLA Modules:
  0.0 543.4 jit_solution(10992987895275895568)
XLA Ops:
  16.2 44.7 %all-gather.9.cloned.1.call-done = bf16[8,147,768]{2,1,0:T(8,128)(2,1)} async-done(((bf16[1,147,768]{2,1,0:T(8,128)(2,1)}), bf16[8,147,768]{2,1,0:T(8,128)(2,1)}) %all-gather.9.cloned.1.call-update) | async-done | bytes 1806352 | tf_op jit(solution)/shard_map/all_gather | solution.py:83
  79.5 44.9 %fusion = bf16[152,768]{1,0:T(8,128)(2,1)S(1)} fusion(bf16[1176,768]{1,0:T(8,128)(2,1)} %convolution_convert_fusion.2), kind=kCustom, calls=%all-reduce-scatter | all-reduce-scatter fusion | flops 933889 | bytes 2040320
  127.8 2.8 concatenate.2
  134.3 47.2 %all-gather.13.cloned.1.call-done = bf16[8,147,768]{2,1,0:T(8,128)(2,1)} async-done(((bf16[1,147,768]{2,1,0:T(8,128)(2,1)}), bf16[8,147,768]{2,1,0:T(8,128)(2,1)}) %all-gather.13.cloned.1.call-update) | async-done | bytes 1806352 | tf_op jit(solution)/shard_map/all_gather | solution.py:220
  181.6 3.3 reshape.427
  184.9 4.0 fusion.98
  188.9 41.1 %all-gather.11.cloned.1.call-done = bf16[8,147,768]{2,1,0:T(8,128)(2,1)} async-done(((bf16[1,147,768]{2,1,0:T(8,128)(2,1)}), bf16[8,147,768]{2,1,0:T(8,128)(2,1)}) %all-gather.11.cloned.1.call-update) | async-done | bytes 1806352 | tf_op jit(solution)/shard_map/all_gather | solution.py:125
  230.0 3.4 reshape.425
  233.3 6.0 %fusion.91 = (bf16[384]{0:T(512)(128)(2,1)}, bf16[1176,384]{1,0:T(8,128)(2,1)S(1)}, f32[1176,384]{1,0:T(8,128)}) fusion(f32[1176,384]{1,0:T(8,128)} %fusion.98, f32[384]{0:T(512)S(1)} %copy-done.51, bf16[1176,768]{1,0:T(8,128)(2,1)} %reshape.425, bf16[768,384]{1,0:T(8,128)(2,1)S(1)} %copy-done), kind=kOutput, calls=%fused_computation.168 | convolution fusion | flops 703567488 | bytes 6914304 | tf_op jit(solution)/shard_map/dot_general | solution.py:126
  242.7 45.4 %fusion.2 = bf16[152,768]{1,0:T(8,128)(2,1)} fusion(bf16[1176,768]{1,0:T(8,128)(2,1)} %convolution_convert_fusion), kind=kCustom, calls=%all-reduce-scatter.2 | all-reduce-scatter fusion | flops 933889 | bytes 2040320
  292.0 4.0 concatenate.4
  300.9 3.9 convolution_convert_fusion.6
  304.8 2.7 convolution_convert_fusion.1
  311.7 37.9 %all-gather.15.cloned.1.call-done = bf16[8,147,768]{2,1,0:T(8,128)(2,1)} async-done(((bf16[1,147,768]{2,1,0:T(8,128)(2,1)}), bf16[8,147,768]{2,1,0:T(8,128)(2,1)}) %all-gather.15.cloned.1.call-update) | async-done | bytes 1806352 | tf_op jit(solution)/shard_map/all_gather | solution.py:235
  349.7 3.4 reshape.429
  353.0 2.8 convolution_convert_fusion.10
  359.6 3.3 fusion.96
  370.9 3.4 fusion.68
  387.1 2.7 convolution_add_fusion.1
  390.5 76.4 %fusion.90 = (bf16[152,768]{1,0:T(8,128)(2,1)S(1)}, bf16[152,768]{1,0:T(8,128)(2,1)S(1)}) fusion(bf16[1176,768]{1,0:T(8,128)(2,1)} %convolution_convert_fusion.1, bf16[1176,768]{1,0:T(8,128)(2,1)S(1)} %fusion.6), kind=kCustom, calls=%all-reduce-scatter.4 | all-reduce-scatter fusion | flops 1867777 | bytes 4080128
  467.0 3.4 collective-permute-start.3
  470.5 4.5 collective-permute-start.1
  480.6 35.2 %psum.63 = bf16[6,768]{1,0:T(8,128)(2,1)S(1)} all-reduce(f32[6,768]{1,0:T(8,128)S(1)} %stack.58), channel_id=1, replica_groups=mesh['dp'=4,'mp'=8] {'mp'}, use_global_device_ids=true, to_apply=%region_21.22 | all-reduce | flops 4608 | bytes 27648 | tf_op jit(solution)/shard_map/psum | solution.py:309
  515.8 10.7 %all-reduce.8 = (bf16[6,768]{1,0:T(8,128)(2,1)S(1)}, bf16[2,96]{1,0:T(2,128)(2,1)S(1)}, bf16[169,3]{0,1:T(4,128)(2,1)S(1)}, bf16[384]{0:T(512)(128)(2,1)S(1)}) all-reduce(bf16[6,768]{1,0:T(8,128)(2,1)S(1)} %psum.63, bf16[2,96]{1,0:T(2,128)(2,1)S(1)} %pad_maximum_fusion.1, ...), channel_id=1, replica_groups=mesh['dp'=4,'mp'=8] {'dp'}, use_global_device_ids=true, to_apply=%region_22.23 | all-reduce | flops 5691 | bytes 22764 | tf_op jit(solution)/shard_map/psum | solution.py:327
  (251 shorter events, 90.7 us)
Async XLA Ops:
  7.2 226.1 %copy-start = (bf16[768,384]{1,0:T(8,128)(2,1)S(1)}, bf16[768,384]{1,0:T(8,128)(2,1)}, u32[]{:S(2)}) copy-start(bf16[768,384]{1,0:T(8,128)(2,1)} %param.27) | copy-start | bytes 1769476
  7.2 53.6 %all-gather.9.cloned.1.call-start = ((), (), s32[]{:S(2)}) async-start(), calls=%async_computation | async-start | bytes 2101248 | tf_op jit(solution)/shard_map/all_gather | solution.py:83
  11.4 170.1 %all-gather.13.cloned.1.call-start = ((), (), s32[]{:S(2)}) async-start(), calls=%async_computation.2 | async-start | bytes 2101248 | tf_op jit(solution)/shard_map/all_gather | solution.py:220
  16.1 54.7 %copy-start.46 = (pred[24]{0:T(512)(128)(4,1)}, pred[24]{0:T(512)(128)(4,1)S(1)}, u32[]{:S(2)}) copy-start(pred[24]{0:T(512)(128)(4,1)S(1)} %broadcast_compare_fusion) | copy-start | bytes 76
  16.2 46.7 %copy-start.20 = (bf16[3,768,96]{1,2,0:T(8,128)(2,1)S(1)}, bf16[3,768,96]{1,2,0:T(8,128)(2,1)}, u32[]{:S(2)}) copy-start(bf16[3,768,96]{1,2,0:T(8,128)(2,1)} %param.20) | copy-start | bytes 1327108
  77.6 48.9 %copy-start.48 = (u32[32]{0:T(128)S(1)}, u32[32]{0:T(128)}, u32[]{:S(2)}) copy-start(u32[32]{0:T(128)} %constant.105) | copy-start | bytes 388
  79.5 51.1 %copy-start.3 = (bf16[147,768]{1,0:T(8,128)(2,1)S(1)}, bf16[147,768]{1,0:T(8,128)(2,1)}, u32[]{:S(2)}) copy-start(bf16[147,768]{1,0:T(8,128)(2,1)} %param.16) | copy-start | bytes 677380
  79.5 51.1 %copy-start.29 = (f32[768]{0:T(1024)S(1)}, f32[768]{0:T(1024)}, u32[]{:S(2)}) copy-start(f32[768]{0:T(1024)} %param.24) | copy-start | bytes 9220
  79.5 53.3 %copy-start.32 = (f32[768]{0:T(1024)S(1)}, f32[768]{0:T(1024)}, u32[]{:S(2)}) copy-start(f32[768]{0:T(1024)} %param.25) | copy-start | bytes 9220
  79.5 53.3 %copy-start.42 = (f32[768]{0:T(1024)S(1)}, f32[768]{0:T(1024)}, u32[]{:S(2)}) copy-start(f32[768]{0:T(1024)} %param.26) | copy-start | bytes 9220
  124.4 3.3 collective-permute-start
  132.8 97.2 %all-gather.11.cloned.1.call-start = ((), (), s32[]{:S(2)}) async-start(), calls=%async_computation.1 | async-start | bytes 2101248 | tf_op jit(solution)/shard_map/all_gather | solution.py:125
  133.8 215.8 %all-gather.15.cloned.1.call-start = ((), (), s32[]{:S(2)}) async-start(), calls=%async_computation.3 | async-start | bytes 2101248 | tf_op jit(solution)/shard_map/all_gather | solution.py:235
  188.9 44.4 %copy-start.51 = (f32[384]{0:T(512)S(1)}, f32[384]{0:T(512)}, u32[]{:S(2)}) copy-start(f32[384]{0:T(512)} %param.28) | copy-start | bytes 4612
  288.9 3.1 collective-permute-start.2
  300.7 230.0 %all-reduce.13.cloned.1.call-start = ((), (), s32[]{:S(2)}) async-start(), calls=%async_computation.4 | async-start | bytes 3538944 | tf_op jit(solution)/shard_map/psum | solution.py:320
  390.5 86.9 %copy-start.25 = (bf16[1,768,96]{1,2,0:T(8,128)(2,1)S(1)}, bf16[1,768,96]{1,2,0:T(8,128)(2,1)}, u32[]{:S(2)}) copy-start(bf16[1,768,96]{1,2,0:T(8,128)(2,1)} %fusion.26) | copy-start | bytes 442372
  467.0 12.3 %collective-permute-start.3 = (bf16[35,768]{1,0:T(8,128)(2,1)S(1)}, bf16[35,768]{1,0:T(8,128)(2,1)S(1)}, u32[]{:S(2)}, u32[]{:S(2)}) collective-permute-start(bf16[35,768]{1,0:T(8,128)(2,1)S(1)} %slice.75), channel_id=1, source_target_pairs={{0,1},{1,2},{2,3},{3,4},{4,5},{5,6},{6,7},{8,9},{9,10},{10,11},{11... | collective-permute-start | bytes 161288
  470.5 57.8 %collective-permute-start.1 = (bf16[35,768]{1,0:T(8,128)(2,1)S(1)}, bf16[35,768]{1,0:T(8,128)(2,1)S(1)}, u32[]{:S(2)}, u32[]{:S(2)}) collective-permute-start(bf16[35,768]{1,0:T(8,128)(2,1)S(1)} %slice.73), channel_id=1, source_target_pairs={{0,1},{1,2},{2,3},{3,4},{4,5},{5,6},{6,7},{8,9},{9,10},{10,11},{11... | collective-permute-start | bytes 161288
  479.2 36.6 %copy-start.44 = (bf16[384]{0:T(512)(128)(2,1)S(1)}, bf16[384]{0:T(512)(128)(2,1)}, u32[]{:S(2)}) copy-start(bf16[384]{0:T(512)(128)(2,1)} %get-tuple-element.43) | copy-start | bytes 2308
  479.3 50.1 %copy-start.7 = (f32[147,768]{1,0:T(8,128)S(1)}, f32[147,768]{1,0:T(8,128)}, u32[]{:S(2)}) copy-start(f32[147,768]{1,0:T(8,128)} %copy-done.6) | copy-start | bytes 1354756
  479.3 50.1 %copy-start.16 = (bf16[147,768]{1,0:T(8,128)(2,1)S(1)}, bf16[147,768]{1,0:T(8,128)(2,1)}, u32[]{:S(2)}) copy-start(bf16[147,768]{1,0:T(8,128)(2,1)} %param.31) | copy-start | bytes 677380
  479.3 50.1 %copy-start.39 = (f32[147]{0:T(256)S(1)}, f32[147]{0:T(256)}, u32[]{:S(2)}) copy-start(f32[147]{0:T(256)} %copy-done.38) | copy-start | bytes 1768
  479.3 50.1 %copy-start.43 = (f32[768]{0:T(1024)S(1)}, f32[768]{0:T(1024)}, u32[]{:S(2)}) copy-start(f32[768]{0:T(1024)} %param.30) | copy-start | bytes 9220
  (42 other events, 143.8 us)
Sparse Core Ops, SparseCore 0:
  11.6 49.2 all-gather.8
  132.9 48.6 all-gather.12
  184.3 45.5 all-gather.10
  300.8 48.8 all-gather.14
  479.5 45.8 all-reduce.12
where the time goes:
time: 553 us; the launch traced here: 543 us
  blocking collectives  213 us (39%)
  waiting for transfers between devices  172 us (31%)
  matrix products  56.3 us (10%)
  local copies, waits for them, and re-layouts  49.3 us (9%)
  other arithmetic  24.9 us (5%)
  between operations  15.5 us (3%)
  starting transfers between devices  12.6 us (2%)
    unnamed x3, blocking collectives  167 us
    all_gather x1, waiting for transfers between devices, shards(): lax.all_gather(mlp_grad.astype(jnp.bfloat16), 'mp', axis=0, tiled=True)  47.2 us
    all_gather x1, waiting for transfers between devices, forward_pass(): rows_one = lax.all_gather(normed_one, 'mp', axis=0, tiled=True)  44.7 us
    all_gather x1, waiting for transfers between devices, forward_pass(): rows_two = lax.all_gather(normed_two, 'mp', axis=0, tiled=True)  41.1 us
    all_gather x1, waiting for transfers between devices, shards(): lax.all_gather(attn_grad.astype(jnp.bfloat16), 'mp', axis=0, tiled=True)  37.9 us
    psum x1, blocking collectives, shards(): small_grads = lax.psum(small_grads, 'mp')  35.2 us
    unnamed x128, local copies, waits for them, and re-layouts  24.7 us
    dot_general x6, matrix products, dot_rows(): lax.dot_general(left, right, (((0,), (0,)), ((), ())), preferred_element_...  15.2 us
  transfers between devices with their start and end apart: 9, of which 5 were waited for; matrix products, arithmetic and copies ran while one was open for 6% of the time, Pallas kernels for 0%

commit v1 on v0

--- a/solution.py
+++ b/solution.py
@@ -306,7 +306,11 @@
             fc2_bias_grad,
         ]
     )
-    small_grads = lax.psum(small_grads, "mp")
+    small_grads = small_grads
+    for hop in (1, 2, 4):
+        small_grads = small_grads + lax.ppermute(
+            small_grads, "mp", [(dev, dev ^ hop) for dev in range(8)]
+        )
     (
         qkv_weight_grad,
         qv_bias_grad,

time: 553 us -> 546 us (0.987)
  blocking collectives: 213 us -> 178 us
  waiting for transfers between devices: 172 us -> 199 us
    psum x1 -> x0, blocking collectives: 35.2 us -> none  [shards(): small_grads = lax.psum(small_grads, 'mp')]
    psum x1, waiting for transfers between devices: 0.01 us -> 18.4 us  [shards(): lax.psum(qkv_weight_grad.astype(jnp.bfloat16), 'dp').astype(jnp.float32)]
    ppermute x0 -> x3, waiting for transfers between devices: none -> 8.23 us  [shards(): lax.ppermute(small_grads, 'mp', [(dev, dev ^ hop) for dev in range(8)])]
    unnamed x128 -> x130, local copies, waits for them, and re-layouts: 24.7 us -> 24.8 us
  transfers between devices with their start and end apart: 9 -> 12, of which waited for: 5 -> 9; matrix products, arithmetic and copies ran while one was open for 6% -> 6% of each run, Pallas kernels for 0% -> 0%
where the time goes in v1:
time: 546 us; the launch traced here: 537 us
  waiting for transfers between devices  199 us (36%)
  blocking collectives  178 us (33%)
  matrix products  56.8 us (10%)
  local copies, waits for them, and re-layouts  47.8 us (9%)
  other arithmetic  24.9 us (5%)
  starting transfers between devices  15.6 us (3%)
  between operations  15.5 us (3%)
    unnamed x3, blocking collectives  167 us
    all_gather x1, waiting for transfers between devices, shards(): lax.all_gather(mlp_grad.astype(jnp.bfloat16), 'mp', axis=0, tiled=True)  47.2 us
    all_gather x1, waiting for transfers between devices, forward_pass(): rows_one = lax.all_gather(normed_one, 'mp', axis=0, tiled=True)  44.7 us
    all_gather x1, waiting for transfers between devices, forward_pass(): rows_two = lax.all_gather(normed_two, 'mp', axis=0, tiled=True)  41.1 us
    all_gather x1, waiting for transfers between devices, shards(): lax.all_gather(attn_grad.astype(jnp.bfloat16), 'mp', axis=0, tiled=True)  37.9 us
    unnamed x130, local copies, waits for them, and re-layouts  24.8 us
    psum x1, waiting for transfers between devices, shards(): lax.psum(qkv_weight_grad.astype(jnp.bfloat16), 'dp').astype(jnp.float32)  18.4 us
    dot_general x6, matrix products, dot_rows(): lax.dot_general(left, right, (((0,), (0,)), ((), ())), preferred_element_...  15.2 us
  transfers between devices with their start and end apart: 12, of which 9 were waited for; matrix products, arithmetic and copies ran while one was open for 6% of the time, Pallas kernels for 0%

profile of v1, /device:TPU:0, one launch (start us, length us, event | category | flops | bytes accessed | tf_op | source)
XLA Modules:
  0.0 537.0 jit_solution(2150522789064452648)
XLA Ops:
  16.2 44.7 %all-gather.9.cloned.1.call-done = bf16[8,147,768]{2,1,0:T(8,128)(2,1)} async-done(((bf16[1,147,768]{2,1,0:T(8,128)(2,1)}), bf16[8,147,768]{2,1,0:T(8,128)(2,1)}) %all-gather.9.cloned.1.call-update) | async-done | bytes 1806352 | tf_op jit(solution)/shard_map/all_gather | solution.py:83
  79.5 44.9 %fusion = bf16[152,768]{1,0:T(8,128)(2,1)S(1)} fusion(bf16[1176,768]{1,0:T(8,128)(2,1)} %convolution_convert_fusion.2), kind=kCustom, calls=%all-reduce-scatter | all-reduce-scatter fusion | flops 933889 | bytes 2040320
  127.8 2.8 concatenate.2
  134.3 47.2 %all-gather.13.cloned.1.call-done = bf16[8,147,768]{2,1,0:T(8,128)(2,1)} async-done(((bf16[1,147,768]{2,1,0:T(8,128)(2,1)}), bf16[8,147,768]{2,1,0:T(8,128)(2,1)}) %all-gather.13.cloned.1.call-update) | async-done | bytes 1806352 | tf_op jit(solution)/shard_map/all_gather | solution.py:220
  181.6 3.3 reshape.427
  184.9 4.0 fusion.98
  188.9 41.1 %all-gather.11.cloned.1.call-done = bf16[8,147,768]{2,1,0:T(8,128)(2,1)} async-done(((bf16[1,147,768]{2,1,0:T(8,128)(2,1)}), bf16[8,147,768]{2,1,0:T(8,128)(2,1)}) %all-gather.11.cloned.1.call-update) | async-done | bytes 1806352 | tf_op jit(solution)/shard_map/all_gather | solution.py:125
  229.9 3.4 reshape.425
  233.3 6.0 %fusion.91 = (bf16[384]{0:T(512)(128)(2,1)}, bf16[1176,384]{1,0:T(8,128)(2,1)S(1)}, f32[1176,384]{1,0:T(8,128)}) fusion(f32[1176,384]{1,0:T(8,128)} %fusion.98, f32[384]{0:T(512)S(1)} %copy-done.53, bf16[1176,768]{1,0:T(8,128)(2,1)} %reshape.425, bf16[768,384]{1,0:T(8,128)(2,1)S(1)} %copy-done), kind=kOutput, calls=%fused_computation.169 | convolution fusion | flops 703567488 | bytes 6914304 | tf_op jit(solution)/shard_map/dot_general | solution.py:126
  242.6 45.4 %fusion.2 = bf16[152,768]{1,0:T(8,128)(2,1)} fusion(bf16[1176,768]{1,0:T(8,128)(2,1)} %convolution_convert_fusion), kind=kCustom, calls=%all-reduce-scatter.2 | all-reduce-scatter fusion | flops 933889 | bytes 2040320
  292.0 4.0 concatenate.4
  300.9 3.9 convolution_convert_fusion.6
  311.7 37.9 %all-gather.15.cloned.1.call-done = bf16[8,147,768]{2,1,0:T(8,128)(2,1)} async-done(((bf16[1,147,768]{2,1,0:T(8,128)(2,1)}), bf16[8,147,768]{2,1,0:T(8,128)(2,1)}) %all-gather.15.cloned.1.call-update) | async-done | bytes 1806352 | tf_op jit(solution)/shard_map/all_gather | solution.py:235
  349.6 3.4 reshape.429
  353.0 2.8 convolution_convert_fusion.10
  359.6 3.9 fusion.96
  371.4 3.5 fusion.68
  389.5 76.4 %fusion.90 = (bf16[152,768]{1,0:T(8,128)(2,1)S(1)}, bf16[152,768]{1,0:T(8,128)(2,1)S(1)}) fusion(bf16[1176,768]{1,0:T(8,128)(2,1)} %convolution_convert_fusion.1, bf16[1176,768]{1,0:T(8,128)(2,1)S(1)} %fusion.6), kind=kCustom, calls=%all-reduce-scatter.4 | all-reduce-scatter fusion | flops 1867777 | bytes 4080128
  465.9 3.4 collective-permute-start.6
  469.4 4.5 collective-permute-start.4
  484.7 2.8 collective-permute-done.1
  489.0 3.6 collective-permute-done.2
  492.6 11.0 %all-reduce.8 = (bf16[6,768]{1,0:T(8,128)(2,1)S(1)}, bf16[2,96]{1,0:T(2,128)(2,1)S(1)}, bf16[169,3]{0,1:T(4,128)(2,1)S(1)}, bf16[384]{0:T(512)(128)(2,1)S(1)}) all-reduce(bf16[6,768]{1,0:T(8,128)(2,1)S(1)} %add_convert_fusion.3, bf16[2,96]{1,0:T(2,128)(2,1)S(1)} %pad_maximum_fusion.1, ...), channel_id=1, replica_groups=mesh['dp'=4,'mp'=8] {'dp'}, use_global_device_ids=true, to_apply=%region_21.22 | all-reduce | flops 5691 | bytes 22764 | tf_op jit(solution)/shard_map/psum | solution.py:331
  505.9 18.4 %all-reduce.13.cloned.1.call-done = (bf16[3,768,96]{1,2,0:T(8,128)(2,1)}, bf16[96,768]{1,0:T(8,128)(2,1)}, bf16[768,384]{1,0:T(8,128)(2,1)}, bf16[384,768]{1,0:T(8,128)(2,1)}) async-done(((bf16[3,768,96]{1,2,0:T(8,128)(2,1)}, bf16[96,768]{1,0:T(8,128)(2,1)}, bf16[768,384]{1,0:T(8,128)(2,1)}, bf16[384,768]{1,0:T(8,128)(2,1)}), (bf16[3,768,96]{1,2,0:T(8,128)(2,1)}, bf16[96,768]{1,0:T(8,128)(2,1)}, ...) | async-done | bytes 1769488 | tf_op jit(solution)/shard_map/psum | solution.py:324
  (261 shorter events, 99.3 us)
Async XLA Ops:
  7.2 226.1 %copy-start = (bf16[768,384]{1,0:T(8,128)(2,1)S(1)}, bf16[768,384]{1,0:T(8,128)(2,1)}, u32[]{:S(2)}) copy-start(bf16[768,384]{1,0:T(8,128)(2,1)} %param.27) | copy-start | bytes 1769476
  7.2 53.6 %all-gather.9.cloned.1.call-start = ((), (), s32[]{:S(2)}) async-start(), calls=%async_computation | async-start | bytes 2101248 | tf_op jit(solution)/shard_map/all_gather | solution.py:83
  11.4 170.1 %all-gather.13.cloned.1.call-start = ((), (), s32[]{:S(2)}) async-start(), calls=%async_computation.2 | async-start | bytes 2101248 | tf_op jit(solution)/shard_map/all_gather | solution.py:220
  16.1 54.7 %copy-start.48 = (pred[24]{0:T(512)(128)(4,1)}, pred[24]{0:T(512)(128)(4,1)S(1)}, u32[]{:S(2)}) copy-start(pred[24]{0:T(512)(128)(4,1)S(1)} %broadcast_compare_fusion) | copy-start | bytes 76
  16.2 46.7 %copy-start.21 = (bf16[3,768,96]{1,2,0:T(8,128)(2,1)S(1)}, bf16[3,768,96]{1,2,0:T(8,128)(2,1)}, u32[]{:S(2)}) copy-start(bf16[3,768,96]{1,2,0:T(8,128)(2,1)} %param.20) | copy-start | bytes 1327108
  77.6 48.9 %copy-start.50 = (u32[32]{0:T(128)S(1)}, u32[32]{0:T(128)}, u32[]{:S(2)}) copy-start(u32[32]{0:T(128)} %constant.105) | copy-start | bytes 388
  79.5 51.1 %copy-start.3 = (bf16[147,768]{1,0:T(8,128)(2,1)S(1)}, bf16[147,768]{1,0:T(8,128)(2,1)}, u32[]{:S(2)}) copy-start(bf16[147,768]{1,0:T(8,128)(2,1)} %param.16) | copy-start | bytes 677380
  79.5 51.1 %copy-start.30 = (f32[768]{0:T(1024)S(1)}, f32[768]{0:T(1024)}, u32[]{:S(2)}) copy-start(f32[768]{0:T(1024)} %param.24) | copy-start | bytes 9220
  79.5 53.3 %copy-start.33 = (f32[768]{0:T(1024)S(1)}, f32[768]{0:T(1024)}, u32[]{:S(2)}) copy-start(f32[768]{0:T(1024)} %param.25) | copy-start | bytes 9220
  79.5 53.3 %copy-start.43 = (f32[768]{0:T(1024)S(1)}, f32[768]{0:T(1024)}, u32[]{:S(2)}) copy-start(f32[768]{0:T(1024)} %param.26) | copy-start | bytes 9220
  124.4 3.3 collective-permute-start.3
  132.8 97.2 %all-gather.11.cloned.1.call-start = ((), (), s32[]{:S(2)}) async-start(), calls=%async_computation.1 | async-start | bytes 2101248 | tf_op jit(solution)/shard_map/all_gather | solution.py:125
  133.8 215.8 %all-gather.15.cloned.1.call-start = ((), (), s32[]{:S(2)}) async-start(), calls=%async_computation.3 | async-start | bytes 2101248 | tf_op jit(solution)/shard_map/all_gather | solution.py:235
  188.9 44.4 %copy-start.53 = (f32[384]{0:T(512)S(1)}, f32[384]{0:T(512)}, u32[]{:S(2)}) copy-start(f32[384]{0:T(512)} %param.28) | copy-start | bytes 4612
  288.8 3.1 collective-permute-start.5
  300.6 223.7 %all-reduce.13.cloned.1.call-start = ((), (), s32[]{:S(2)}) async-start(), calls=%async_computation.4 | async-start | bytes 3538944 | tf_op jit(solution)/shard_map/psum | solution.py:324
  389.4 86.9 %copy-start.26 = (bf16[1,768,96]{1,2,0:T(8,128)(2,1)S(1)}, bf16[1,768,96]{1,2,0:T(8,128)(2,1)}, u32[]{:S(2)}) copy-start(bf16[1,768,96]{1,2,0:T(8,128)(2,1)} %fusion.26) | copy-start | bytes 442372
  465.9 12.3 %copy-start.45 = (bf16[3,32]{1,0:T(4,128)(2,1)S(1)}, bf16[3,32]{1,0:T(4,128)(2,1)}, u32[]{:S(2)}) copy-start(bf16[3,32]{1,0:T(4,128)(2,1)} %get-tuple-element.62) | copy-start | bytes 580
  465.9 12.3 %collective-permute-start.6 = (bf16[35,768]{1,0:T(8,128)(2,1)S(1)}, bf16[35,768]{1,0:T(8,128)(2,1)S(1)}, u32[]{:S(2)}, u32[]{:S(2)}) collective-permute-start(bf16[35,768]{1,0:T(8,128)(2,1)S(1)} %slice.75), channel_id=1, source_target_pairs={{0,1},{1,2},{2,3},{3,4},{4,5},{5,6},{6,7},{8,9},{9,10},{10,11},{11... | collective-permute-start | bytes 161288
  469.4 15.0 %collective-permute-start.4 = (bf16[35,768]{1,0:T(8,128)(2,1)S(1)}, bf16[35,768]{1,0:T(8,128)(2,1)S(1)}, u32[]{:S(2)}, u32[]{:S(2)}) collective-permute-start(bf16[35,768]{1,0:T(8,128)(2,1)S(1)} %slice.73), channel_id=1, source_target_pairs={{0,1},{1,2},{2,3},{3,4},{4,5},{5,6},{6,7},{8,9},{9,10},{10,11},{11... | collective-permute-start | bytes 161288
  479.0 13.6 %copy-start.46 = (bf16[384]{0:T(512)(128)(2,1)S(1)}, bf16[384]{0:T(512)(128)(2,1)}, u32[]{:S(2)}) copy-start(bf16[384]{0:T(512)(128)(2,1)} %get-tuple-element.43) | copy-start | bytes 2308
  479.5 4.2 collective-permute-start
  483.7 3.8 collective-permute-start.1
  487.6 5.0 collective-permute-start.2
  (46 other events, 165.9 us)
Sparse Core Ops, SparseCore 0:
  11.6 49.2 all-gather.8
  132.9 48.6 all-gather.12
  184.3 45.5 all-gather.10
  300.7 48.8 all-gather.14
  478.4 45.8 all-reduce.12
